TPU v7x, 32 devices: a whole 2x2x4 slice. The times are simulated.
32 devices in a mesh: rows: 32 (over z, y, x, core).
Axes of the slice: x: 2, y: 2, z: 4, core: 2. Of those that a mesh axis runs over, the one named last changes fastest.
Arguments:
- live_blocks: int32 [32], P('rows'), may hold values from 16 to 48, as said below
- tile_columns: int32 [1536, 12], P('rows'), may hold values from 0 to 143, as said below
- send_lists: int32 [32, 6, 16], P('rows'), may hold values from 0 to 47, as said below
- tiles: bfloat16 [1536, 12, 128, 128], P('rows'), may hold values from -0.09375 to 0.09375
- filter_coeffs: float32 [4], replicated, may hold values from 0.3 to 1.5
- start_block: bfloat16 [1536, 32, 128], P('rows')
- previous_block: float32 [1536, 32, 128], P('rows')
Outputs:
- basis: float32 [1536, 32, 128], P('rows')
Inputs may be any that keep to these rules, and one draw needn't show every extreme that they name: `live_blocks`: at least one device has 48 live slots and one has 16. `tile_columns`: entry k = 0 of row b is b's own slot; other entries are a live own slot of the device or a ghost slot 48 + o * 16 + s. `send_lists`: every entry is below the sending device's live count.
All inputs are finite; a program needn't handle non-finite values.
Results may differ from a plain program's by a relative error of at most 0.0028.
Values may be sent and summed in bfloat16 or wider, within the bound.
A program may use at most 128 MiB of HBM per device.

v0:
```python
import functools
import math

import jax
import jax.numpy as jnp
from jax import lax
from jax.experimental import pallas as pl
from jax.experimental.pallas import tpu as pltpu
from jax.sharding import PartitionSpec as P

MESH = pl.DeviceIdType.MESH
HIGHEST = lax.Precision.HIGHEST
GROUP = 8
UNROLL = 3
CHUNKS = 8
F32, BF16 = jnp.float32, jnp.bfloat16


def shift_amount(which):
    return (which // 2 + 1) * (1 if which % 2 == 0 else -1)


def iota(axis):
    return lax.broadcasted_iota(jnp.int32, (32, 128), axis)


def split(value):
    high = value.astype(BF16)
    return high, (value - high.astype(F32)).astype(BF16)


def eliminate(matrix, full):
    rows, lanes = iota(0), iota(1)
    for j in range(32):
        row = matrix[j : j + 1, :]
        column = matrix[:, j : j + 1]
        pivot = matrix[j : j + 1, j : j + 1]
        keep = (rows != j) if full else (rows > j)
        matrix = matrix - jnp.where(keep, column * (row / pivot), 0.0)
    diagonal = jnp.sum(jnp.where(rows == lanes, matrix, 0.0), axis=1, keepdims=True)
    return matrix, diagonal


def pack(total):
    folded = total + pltpu.roll(total, 64, 1)
    return jnp.where(iota(1)[:16] < 64, folded[:16], folded[16:])


def unpack(packed):
    return jnp.concatenate([packed, pltpu.roll(packed, 64, 1)], axis=0)


def kernel(
    n, scale, live_ref, cols_ref, sends_ref, coeff_ref, start_ref, tiles_hbm, prev_hbm, out_ref,
    tiles, prev, ext_a0, ext_b0, ext_a1, ext_b1, ext_a2, ext_b2, own_a1, own_b1, own_a2, own_b2,
    outgoing, first, accum, y_high, y_low, inverse, mine, within, across,
    tile_sem, prev_sem, halo_send, halo_recv, sum_send, sum_recv,
):
    capacity = start_ref.shape[0]
    fan = cols_ref.shape[0]
    size = capacity // CHUNKS
    neighbours, _, count = sends_ref.shape
    groups = n // GROUP
    me = lax.axis_index("rows")
    ext = [[ext_a0, ext_b0], [ext_a1, ext_b1], [ext_a2, ext_b2]]
    own = [None, [own_a1, own_b1], [own_a2, own_b2]]
    live = live_ref[0]

    tile_copies = []
    for c in range(CHUNKS):
        piece = pl.ds(c * size, size)
        copy = pltpu.make_async_copy(tiles_hbm.at[piece], tiles.at[piece], tile_sem.at[c])
        copy.start()
        tile_copies.append(copy)
    prev_copy = pltpu.make_async_copy(prev_hbm, prev, prev_sem)
    prev_copy.start()

    def halo_target(which):
        return lax.rem(me + shift_amount(which) + n, n)

    def group_mate(k):
        return me // GROUP * GROUP + lax.rem(lax.rem(me, GROUP) + k, GROUP)

    def other_group(k):
        return lax.rem(me + k * GROUP, n)

    barrier = pltpu.get_barrier_semaphore()
    partners = [halo_target(w) for w in range(neighbours)]
    partners += [group_mate(k) for k in range(1, GROUP)]
    partners += [other_group(k) for k in range(1, groups)]
    for partner in partners:
        pl.semaphore_signal(barrier, inc=1, device_id=(partner,), device_id_type=MESH)

    def gather(step, half, which):
        base = ((step * 2 + half) * neighbours + which) * count
        for s in range(count):
            index = sends_ref[which, 0, s]
            if step == 0:
                outgoing[base + s] = start_ref[index, half * 16 : half * 16 + 16]
            else:
                outgoing[base + s] = own[step][half][index]

    def halo_copy(step, half, which):
        slot = (step * 2 + half) * neighbours + which
        return pltpu.make_async_remote_copy(
            src_ref=outgoing.at[pl.ds(slot * count, count)],
            dst_ref=ext[step][half].at[pl.ds(capacity + which * count, count)],
            send_sem=halo_send.at[slot],
            recv_sem=halo_recv.at[slot],
            device_id=(halo_target(which),),
            device_id_type=MESH,
        )

    order = (4, 5, 2, 3, 0, 1)
    for half in range(2):
        for which in order:
            gather(0, half, which)
    pl.semaphore_wait(barrier, len(partners))
    for which in order:
        halo_copy(0, 0, which).start()

    def mask(b):
        return jnp.where(b < live, 1.0, 0.0).astype(F32)

    def fill(b, carry):
        value = (start_ref[b].astype(F32) * mask(b)).astype(BF16)
        ext_a0[b] = value[:16]
        ext_b0[b] = value[16:]
        return carry

    lax.fori_loop(0, capacity, fill, 0, unroll=4)

    def within_copy(which, k):
        slot = which * (GROUP - 1 + groups - 1) + k - 1
        return pltpu.make_async_remote_copy(
            src_ref=mine.at[2 * which],
            dst_ref=within.at[which * (GROUP - 1) + k - 1],
            send_sem=sum_send.at[slot],
            recv_sem=sum_recv.at[slot],
            device_id=(group_mate(k),),
            device_id_type=MESH,
        )

    def across_copy(which, k):
        slot = which * (GROUP - 1 + groups - 1) + GROUP - 1 + k - 1
        return pltpu.make_async_remote_copy(
            src_ref=mine.at[2 * which + 1],
            dst_ref=across.at[which * (groups - 1) + k - 1],
            send_sem=sum_send.at[slot],
            recv_sem=sum_recv.at[slot],
            device_id=(other_group(k),),
            device_id_type=MESH,
        )

    def sum_start(which, value):
        mine[2 * which] = value
        for k in range(1, GROUP):
            within_copy(which, k).start()

    def sum_middle(which):
        total = mine[2 * which]
        for k in range(1, GROUP):
            within_copy(which, k).wait_recv()
            total += within[which * (GROUP - 1) + k - 1]
        mine[2 * which + 1] = total
        for k in range(1, groups):
            across_copy(which, k).start()

    def sum_end(which):
        total = mine[2 * which + 1]
        for k in range(1, groups):
            across_copy(which, k).wait_recv()
            total += across[which * (groups - 1) + k - 1]
        return total

    rows_dot = functools.partial(
        lax.dot_general, dimension_numbers=(((1,), (1,)), ((), ())), preferred_element_type=F32
    )

    prev_copy.wait()

    def prev_gram(pair, total):
        left, right = [], []
        for b in (2 * pair, 2 * pair + 1):
            high, low = split(prev[b] * mask(b))
            y_high[b, :32] = high
            y_low[b, :32] = low
            left.append(jnp.concatenate([high, low], axis=0))
            right.append(jnp.concatenate([high, high, low, low], axis=0))
        return total + rows_dot(
            jnp.concatenate(left, axis=1), jnp.concatenate(right, axis=1)
        )

    total = lax.fori_loop(0, capacity // 2, prev_gram, jnp.zeros((64, 128), F32), unroll=2)
    sum_start(0, pack(total[:32] + total[32:]))
    for which in order:
        halo_copy(0, 0, which).wait_send()
    for which in order:
        halo_copy(0, 1, which).start()

    def products(step, half, b):
        vectors = ext[step][half]
        picked = [
            jnp.concatenate([vectors[cols_ref[k, row]] for k in range(fan)], axis=1)
            for row in (b, b + 1)
        ]
        result = jnp.dot(
            jnp.concatenate(picked, axis=0),
            jnp.concatenate([tiles[b], tiles[b + 1]], axis=1),
            preferred_element_type=F32,
        )
        return result[:16, :128] * mask(b), result[16:, 128:] * mask(b + 1)

    c0, c1, c2, c3 = (coeff_ref[i] for i in range(4))

    def first_step(half, b):
        for i, result in enumerate(products(0, half, b)):
            rounded = result.astype(BF16)
            first[half, b + i] = result
            own[1][half][b + i] = rounded
            ext[1][half][b + i] = rounded

    def second_step(half, b):
        for i, result in enumerate(products(1, half, b)):
            before = ext[0][half][b + i].astype(F32)
            one = first[half, b + i]
            result = 2.0 * result - before
            rounded = result.astype(BF16)
            own[2][half][b + i] = rounded
            ext[2][half][b + i] = rounded
            accum[half, b + i] = c0 * before + (c1 - c3) * one + c2 * result

    def third_step(half, b):
        rows = slice(32 + 16 * half, 48 + 16 * half)
        for i, result in enumerate(products(2, half, b)):
            high, low = split(accum[half, b + i] + (2.0 * c3) * result)
            y_high[b + i, rows] = high
            y_low[b + i, rows] = low

    def await_halo(step, half):
        for which in order:
            halo_copy(step, half, which).wait_recv()

    def loop(body, lower, upper):
        def pair(i, carry):
            body(lower + 2 * i)
            return carry

        lax.fori_loop(0, (upper - lower) // 2, pair, 0, unroll=UNROLL)

    for half in range(2):
        await_halo(0, half)
        for c in range(CHUNKS):
            if half == 0:
                tile_copies[c].wait()
                loop(functools.partial(first_step, half), c * size, (c + 1) * size)
        if half == 1:
            loop(functools.partial(first_step, half), 0, capacity)
        for which in order:
            gather(1, half, which)
            halo_copy(1, half, which).start()
    sum_middle(0)
    for half in range(2):
        await_halo(1, half)
        loop(functools.partial(second_step, half), 0, capacity)
        for which in order:
            gather(2, half, which)
            halo_copy(2, half, which).start()

    rows, lanes = iota(0), iota(1)
    gram = unpack(sum_end(0))
    matrix = jnp.where(lanes < 32, gram, jnp.where(lanes == rows + 64, 1.0, 0.0))
    matrix, diagonal = eliminate(matrix, True)
    middle = (lanes >= 32) & (lanes < 64)
    inverse[...] = jnp.where(middle, pltpu.roll(matrix / diagonal, 96, 1), 0.0)

    await_halo(2, 0)
    loop(functools.partial(third_step, 0), 0, capacity)
    await_halo(2, 1)

    def last_step(pair, total):
        left, right = [], []
        third_step(1, 2 * pair)
        for b in (2 * pair, 2 * pair + 1):
            left.append(jnp.concatenate([y_high[b, 32:64], y_low[b, 32:64]], axis=0))
            right.append(jnp.concatenate([y_high[b], y_low[b]], axis=0))
        return total + rows_dot(
            jnp.concatenate(left, axis=1), jnp.concatenate(right, axis=1)
        )

    total = lax.fori_loop(0, capacity // 2, last_step, jnp.zeros((64, 128), F32), unroll=UNROLL)
    sum_start(1, pack(total[:32] + total[32:]))
    sum_middle(1)
    sums = unpack(sum_end(1))

    cross = jnp.where(lanes < 32, sums, 0.0)
    below = jnp.zeros((96, 128), F32)
    coeff = jnp.dot(
        cross, jnp.concatenate([inverse[...], below], axis=0),
        precision=HIGHEST, preferred_element_type=F32,
    )
    removed = rows_dot(
        coeff, jnp.concatenate([pltpu.roll(cross, 32, 1), below], axis=0), precision=HIGHEST
    )
    matrix = jnp.where(
        lanes < 32,
        pltpu.roll(sums, 96, 1) - removed,
        jnp.where(lanes < 64, -coeff, jnp.where(lanes == rows + 64, 1.0, 0.0)),
    )
    matrix, diagonal = eliminate(matrix, False)
    factor = pltpu.roll(matrix * (scale * lax.rsqrt(diagonal)), 96, 1)
    factor = jnp.where(lanes < 64, factor, 0.0)
    high = factor.astype(BF16).astype(F32)
    both = jnp.where(lanes < 64, high, pltpu.roll(factor - high, 64, 1)).astype(BF16)
    both = jnp.concatenate([both, both], axis=1)

    def finish(pair, carry):
        stacked = []
        for b in (2 * pair, 2 * pair + 1):
            h, l = y_high[b], y_low[b]
            stacked.append(jnp.concatenate([h, h, l, l], axis=0))
        result = jnp.dot(
            both, jnp.concatenate(stacked, axis=1), preferred_element_type=F32
        )
        out_ref[2 * pair] = result[:, :128]
        out_ref[2 * pair + 1] = result[:, 128:]
        return carry

    lax.fori_loop(0, capacity // 2, finish, 0, unroll=2)

    for step in range(3):
        for half in range(2):
            for which in order:
                if (step, half) != (0, 0):
                    halo_copy(step, half, which).wait_send()
    for which in range(2):
        for k in range(1, GROUP):
            within_copy(which, k).wait_send()
        for k in range(1, groups):
            across_copy(which, k).wait_send()


def shards(
    live_blocks, tile_columns, send_lists, tiles, filter_coeffs, start_block, previous_block
):
    n = lax.axis_size("rows")
    capacity, vectors, rows = start_block.shape
    fan = tile_columns.shape[1]
    _, neighbours, count = send_lists.shape
    groups = n // GROUP
    sums = 2 * (GROUP - 1 + groups - 1)
    smem = pl.BlockSpec(memory_space=pltpu.SMEM)
    vmem = pl.BlockSpec(memory_space=pltpu.VMEM)
    hbm = pl.BlockSpec(memory_space=pl.ANY)
    half = vectors // 2
    field = pltpu.VMEM((capacity, half, rows), BF16)
    extended = pltpu.VMEM((capacity + neighbours * count, half, rows), BF16)
    wide = pltpu.VMEM((2, capacity, half, rows), F32)
    stacked = pltpu.VMEM((capacity, 2 * vectors, rows), BF16)
    scale = math.sqrt(capacity * n * rows)
    return pl.pallas_call(
        functools.partial(kernel, n, scale),
        out_shape=jax.ShapeDtypeStruct((capacity, vectors, rows), F32),
        in_specs=[smem, smem, smem, smem, vmem, hbm, hbm],
        out_specs=vmem,
        scratch_shapes=[
            pltpu.VMEM((capacity, fan * rows, rows), BF16),
            pltpu.VMEM((capacity, vectors, rows), F32),
            *[extended] * 6,
            *[field] * 4,
            pltpu.VMEM((6 * neighbours * count, half, rows), BF16),
            wide,
            wide,
            stacked,
            stacked,
            pltpu.VMEM((vectors, 128), F32),
            pltpu.VMEM((4, 16, 128), F32),
            pltpu.VMEM((2 * (GROUP - 1), 16, 128), F32),
            pltpu.VMEM((2 * (groups - 1), 16, 128), F32),
            pltpu.SemaphoreType.DMA((CHUNKS,)),
            pltpu.SemaphoreType.DMA,
            pltpu.SemaphoreType.DMA((6 * neighbours,)),
            pltpu.SemaphoreType.DMA((6 * neighbours,)),
            pltpu.SemaphoreType.DMA((sums,)),
            pltpu.SemaphoreType.DMA((sums,)),
        ],
        compiler_params=pltpu.CompilerParams(
            collective_id=0, has_side_effects=True, vmem_limit_bytes=64 * 1024 * 1024
        ),
        name="filtered_step",
    )(
        live_blocks,
        tile_columns.T,
        jnp.transpose(send_lists, (1, 0, 2)),
        filter_coeffs,
        start_block,
        tiles.reshape(capacity, fan * rows, rows),
        previous_block,
    )


def solution(mesh):
    return jax.shard_map(
        shards,
        mesh=mesh,
        in_specs=(
            P("rows"),
            P("rows", None),
            P("rows", None, None),
            P("rows", None, None, None),
            P(),
            P("rows", None, None),
            P("rows", None, None),
        ),
        out_specs=P("rows", None, None),
        check_vma=False,
    )
```

profile of v0, /device:TPU:0, one launch (start us, length us, event | category | flops | bytes accessed | tf_op | source)
XLA Modules:
  0.0 71.1 jit_solution(12189531616777545005)
XLA Ops:
  0.7 68.4 %filtered_step.1 = f32[48,32,128]{2,1,0:T(8,128)} custom-call(s32[1]{0:T(128)S(6)} %copy.9.live_ref, s32[12,48]{1,0:T(8,128)} %bitcast.4, s32[6,1,16]{2,1,0:T(1,128)} %bitcast.5, f32[4]{0:T(128)} %coeff_ref.1, bf16[48,32,128]{2,1,0:T(8,128)(2,1)} %start_ref.1, bf16[48,1536,128]{2,1,0:T(8,128)(2,1)} %bitcast.3, f32[48,32,128]{2,1,0:T(8,128)} %prev_hbm.1), custom_call_target="tpu_custom_call" | custom-call | tf_op jit(solution)/shard_map/filtered_step/pallas_call | solution.py:361
  69.0 2.1 %copy.10 = f32[48,32,128]{2,1,0:T(8,128)} copy(f32[48,32,128]{2,1,0:T(8,128)} %filtered_step.1) | data formatting | bytes 1572864
where the time goes:
time: 71.3 us; the launch traced here: 71.1 us
  Pallas kernels  68.4 us (96%)
  local copies, waits for them, and re-layouts  2.06 us (3%)
    pallas_call x1, Pallas kernels, shards(): pl.pallas_call(functools.partial(kernel, n, scale), out_shape=jax.ShapeDt...  68.4 us
    unnamed x1, local copies, waits for them, and re-layouts  2.06 us

commit v1 on v0

--- a/solution.py
+++ b/solution.py
@@ -11,6 +11,7 @@
 MESH = pl.DeviceIdType.MESH
 HIGHEST = lax.Precision.HIGHEST
 GROUP = 8
+PIVOTS = 8
 UNROLL = 3
 CHUNKS = 8
 F32, BF16 = jnp.float32, jnp.bfloat16
@@ -30,14 +31,22 @@
 
 
 def eliminate(matrix, full):
-    rows, lanes = iota(0), iota(1)
-    for j in range(32):
-        row = matrix[j : j + 1, :]
-        column = matrix[:, j : j + 1]
-        pivot = matrix[j : j + 1, j : j + 1]
-        keep = (rows != j) if full else (rows > j)
-        matrix = matrix - jnp.where(keep, column * (row / pivot), 0.0)
-    diagonal = jnp.sum(jnp.where(rows == lanes, matrix, 0.0), axis=1, keepdims=True)
+    rows = iota(0)
+    diagonal = jnp.zeros((32, 128), F32)
+    for start in range(0, 32, PIVOTS):
+        columns = [
+            jnp.broadcast_to(matrix[:, j : j + 1], (32, 128))
+            for j in range(start, start + PIVOTS)
+        ]
+        for p in range(PIVOTS):
+            j = start + p
+            row, column = matrix[j : j + 1, :], columns[p]
+            keep = (rows != j) if full else (rows > j)
+            factor = jnp.where(keep, column * (1.0 / column[j : j + 1, :]), 0.0)
+            diagonal = jnp.where(rows == j, column, diagonal)
+            matrix = matrix - factor * row
+            for q in range(p + 1, PIVOTS):
+                columns[q] = columns[q] - factor * columns[q][j : j + 1, :]
     return matrix, diagonal
 
 
@@ -66,14 +75,14 @@
     own = [None, [own_a1, own_b1], [own_a2, own_b2]]
     live = live_ref[0]
 
+    prev_copy = pltpu.make_async_copy(prev_hbm, prev, prev_sem)
+    prev_copy.start()
     tile_copies = []
     for c in range(CHUNKS):
         piece = pl.ds(c * size, size)
         copy = pltpu.make_async_copy(tiles_hbm.at[piece], tiles.at[piece], tile_sem.at[c])
         copy.start()
         tile_copies.append(copy)
-    prev_copy = pltpu.make_async_copy(prev_hbm, prev, prev_sem)
-    prev_copy.start()
 
     def halo_target(which):
         return lax.rem(me + shift_amount(which) + n, n)
@@ -259,7 +268,16 @@
         for which in order:
             gather(1, half, which)
             halo_copy(1, half, which).start()
-    sum_middle(0)
+        if half == 0:
+            sum_middle(0)
+
+    rows, lanes = iota(0), iota(1)
+    gram = unpack(sum_end(0))
+    matrix = jnp.where(lanes < 32, gram, jnp.where(lanes == rows + 64, 1.0, 0.0))
+    matrix, diagonal = eliminate(matrix, True)
+    middle = (lanes >= 32) & (lanes < 64)
+    inverse[...] = jnp.where(middle, pltpu.roll(matrix / diagonal, 96, 1), 0.0)
+
     for half in range(2):
         await_halo(1, half)
         loop(functools.partial(second_step, half), 0, capacity)
@@ -267,28 +285,34 @@
             gather(2, half, which)
             halo_copy(2, half, which).start()
 
-    rows, lanes = iota(0), iota(1)
-    gram = unpack(sum_end(0))
-    matrix = jnp.where(lanes < 32, gram, jnp.where(lanes == rows + 64, 1.0, 0.0))
-    matrix, diagonal = eliminate(matrix, True)
-    middle = (lanes >= 32) & (lanes < 64)
-    inverse[...] = jnp.where(middle, pltpu.roll(matrix / diagonal, 96, 1), 0.0)
-
     await_halo(2, 0)
+    span = 2 * UNROLL
+
+    def third_group(half, group):
+        for i in range(UNROLL):
+            third_step(half, group * span + 2 * i)
+
+    def filtered_gram(group, total):
+        for i in range(UNROLL):
+            left, right = [], []
+            for b in (group * span + 2 * i, group * span + 2 * i + 1):
+                left.append(jnp.concatenate([y_high[b, 32:64], y_low[b, 32:64]], axis=0))
+                right.append(jnp.concatenate([y_high[b], y_low[b]], axis=0))
+            total += rows_dot(
+                jnp.concatenate(left, axis=1), jnp.concatenate(right, axis=1)
+            )
+        return total
+
+    def last_group(group, total):
+        total = filtered_gram(group - 1, total)
+        third_group(1, group)
+        return total
+
     loop(functools.partial(third_step, 0), 0, capacity)
     await_halo(2, 1)
-
-    def last_step(pair, total):
-        left, right = [], []
-        third_step(1, 2 * pair)
-        for b in (2 * pair, 2 * pair + 1):
-            left.append(jnp.concatenate([y_high[b, 32:64], y_low[b, 32:64]], axis=0))
-            right.append(jnp.concatenate([y_high[b], y_low[b]], axis=0))
-        return total + rows_dot(
-            jnp.concatenate(left, axis=1), jnp.concatenate(right, axis=1)
-        )
-
-    total = lax.fori_loop(0, capacity // 2, last_step, jnp.zeros((64, 128), F32), unroll=UNROLL)
+    third_group(1, 0)
+    total = lax.fori_loop(1, capacity // span, last_group, jnp.zeros((64, 128), F32))
+    total = filtered_gram(capacity // span - 1, total)
     sum_start(1, pack(total[:32] + total[32:]))
     sum_middle(1)
     sums = unpack(sum_end(1))

time: 71.3 us -> 66.1 us (0.927)
  Pallas kernels: 68.4 us -> 63.2 us
    pallas_call x1, Pallas kernels: 68.4 us -> 63.2 us  [shards(): pl.pallas_call(functools.partial(kernel, n, scale), out_shape=jax.ShapeDt...]
where the time goes in v1:
time: 66.1 us; the launch traced here: 65.9 us
  Pallas kernels  63.2 us (96%)
  local copies, waits for them, and re-layouts  2.06 us (3%)
    pallas_call x1, Pallas kernels, shards(): pl.pallas_call(functools.partial(kernel, n, scale), out_shape=jax.ShapeDt...  63.2 us
    unnamed x1, local copies, waits for them, and re-layouts  2.06 us

profile of v1, /device:TPU:0, one launch (start us, length us, event | category | flops | bytes accessed | tf_op | source)
XLA Modules:
  0.0 65.9 jit_solution(5384005521926779682)
XLA Ops:
  0.7 63.2 %filtered_step.1 = f32[48,32,128]{2,1,0:T(8,128)} custom-call(s32[1]{0:T(128)S(6)} %copy.9.live_ref, s32[12,48]{1,0:T(8,128)} %bitcast.4, s32[6,1,16]{2,1,0:T(1,128)} %bitcast.5, f32[4]{0:T(128)} %coeff_ref.1, bf16[48,32,128]{2,1,0:T(8,128)(2,1)} %start_ref.1, bf16[48,1536,128]{2,1,0:T(8,128)(2,1)} %bitcast.3, f32[48,32,128]{2,1,0:T(8,128)} %prev_hbm.1), custom_call_target="tpu_custom_call" | custom-call | tf_op jit(solution)/shard_map/filtered_step/pallas_call | solution.py:385
  63.8 2.1 %copy.10 = f32[48,32,128]{2,1,0:T(8,128)} copy(f32[48,32,128]{2,1,0:T(8,128)} %filtered_step.1) | data formatting | bytes 1572864

commit v2 on v1

--- a/solution.py
+++ b/solution.py
@@ -12,6 +12,7 @@
 HIGHEST = lax.Precision.HIGHEST
 GROUP = 8
 PIVOTS = 8
+PARTS = 4
 UNROLL = 3
 CHUNKS = 8
 F32, BF16 = jnp.float32, jnp.bfloat16
@@ -60,10 +61,11 @@
 
 
 def kernel(
-    n, scale, live_ref, cols_ref, sends_ref, coeff_ref, start_ref, tiles_hbm, prev_hbm, out_ref,
+    n, scale, live_ref, cols_ref, sends_ref, coeff_ref, start_ref, tiles_hbm, prev_hbm,
+    factor_ref, high_hbm, low_hbm,
     tiles, prev, ext_a0, ext_b0, ext_a1, ext_b1, ext_a2, ext_b2, own_a1, own_b1, own_a2, own_b2,
     outgoing, first, accum, y_high, y_low, inverse, mine, within, across,
-    tile_sem, prev_sem, halo_send, halo_recv, sum_send, sum_recv,
+    tile_sem, prev_sem, out_sem, halo_send, halo_recv, sum_send, sum_recv,
 ):
     capacity = start_ref.shape[0]
     fan = cols_ref.shape[0]
@@ -114,9 +116,20 @@
         return pltpu.make_async_remote_copy(
             src_ref=outgoing.at[pl.ds(slot * count, count)],
             dst_ref=ext[step][half].at[pl.ds(capacity + which * count, count)],
-            send_sem=halo_send.at[slot],
-            recv_sem=halo_recv.at[slot],
+            send_sem=halo_send.at[step * 2 + half],
+            recv_sem=halo_recv.at[step * 2 + half],
             device_id=(halo_target(which),),
+            device_id_type=MESH,
+        )
+
+    def halo_whole(step, half):
+        ghosts = neighbours * count
+        return pltpu.make_async_remote_copy(
+            src_ref=outgoing.at[pl.ds((step * 2 + half) * ghosts, ghosts)],
+            dst_ref=ext[step][half].at[pl.ds(capacity, ghosts)],
+            send_sem=halo_send.at[step * 2 + half],
+            recv_sem=halo_recv.at[step * 2 + half],
+            device_id=(halo_target(0),),
             device_id_type=MESH,
         )
 
@@ -140,24 +153,34 @@
     lax.fori_loop(0, capacity, fill, 0, unroll=4)
 
     def within_copy(which, k):
-        slot = which * (GROUP - 1 + groups - 1) + k - 1
         return pltpu.make_async_remote_copy(
             src_ref=mine.at[2 * which],
             dst_ref=within.at[which * (GROUP - 1) + k - 1],
-            send_sem=sum_send.at[slot],
-            recv_sem=sum_recv.at[slot],
+            send_sem=sum_send.at[2 * which],
+            recv_sem=sum_recv.at[2 * which],
             device_id=(group_mate(k),),
             device_id_type=MESH,
         )
 
     def across_copy(which, k):
-        slot = which * (GROUP - 1 + groups - 1) + GROUP - 1 + k - 1
         return pltpu.make_async_remote_copy(
             src_ref=mine.at[2 * which + 1],
             dst_ref=across.at[which * (groups - 1) + k - 1],
+            send_sem=sum_send.at[2 * which + 1],
+            recv_sem=sum_recv.at[2 * which + 1],
+            device_id=(other_group(k),),
+            device_id_type=MESH,
+        )
+
+    def sum_whole(which, landing):
+        peers = landing.shape[0] // 2
+        slot = 2 * which + (0 if landing is within else 1)
+        return pltpu.make_async_remote_copy(
+            src_ref=landing.at[pl.ds(which * peers, peers)],
+            dst_ref=landing.at[pl.ds(which * peers, peers)],
             send_sem=sum_send.at[slot],
             recv_sem=sum_recv.at[slot],
-            device_id=(other_group(k),),
+            device_id=(group_mate(1),),
             device_id_type=MESH,
         )
 
@@ -168,8 +191,8 @@
 
     def sum_middle(which):
         total = mine[2 * which]
+        sum_whole(which, within).wait_recv()
         for k in range(1, GROUP):
-            within_copy(which, k).wait_recv()
             total += within[which * (GROUP - 1) + k - 1]
         mine[2 * which + 1] = total
         for k in range(1, groups):
@@ -177,8 +200,8 @@
 
     def sum_end(which):
         total = mine[2 * which + 1]
+        sum_whole(which, across).wait_recv()
         for k in range(1, groups):
-            across_copy(which, k).wait_recv()
             total += across[which * (groups - 1) + k - 1]
         return total
 
@@ -202,8 +225,7 @@
 
     total = lax.fori_loop(0, capacity // 2, prev_gram, jnp.zeros((64, 128), F32), unroll=2)
     sum_start(0, pack(total[:32] + total[32:]))
-    for which in order:
-        halo_copy(0, 0, which).wait_send()
+    halo_whole(0, 0).wait_send()
     for which in order:
         halo_copy(0, 1, which).start()
 
@@ -247,8 +269,7 @@
             y_low[b + i, rows] = low
 
     def await_halo(step, half):
-        for which in order:
-            halo_copy(step, half, which).wait_recv()
+        halo_whole(step, half).wait_recv()
 
     def loop(body, lower, upper):
         def pair(i, carry):
@@ -313,7 +334,13 @@
     third_group(1, 0)
     total = lax.fori_loop(1, capacity // span, last_group, jnp.zeros((64, 128), F32))
     total = filtered_gram(capacity // span - 1, total)
+    out_copies = [
+        pltpu.make_async_copy(y_high, high_hbm, out_sem.at[0]),
+        pltpu.make_async_copy(y_low, low_hbm, out_sem.at[1]),
+    ]
     sum_start(1, pack(total[:32] + total[32:]))
+    for copy in out_copies:
+        copy.start()
     sum_middle(1)
     sums = unpack(sum_end(1))
 
@@ -336,7 +363,7 @@
     factor = jnp.where(lanes < 64, factor, 0.0)
     high = factor.astype(BF16).astype(F32)
     both = jnp.where(lanes < 64, high, pltpu.roll(factor - high, 64, 1)).astype(BF16)
-    both = jnp.concatenate([both, both], axis=1)
+    factor_ref[...] = jnp.concatenate([both, both], axis=1)
 
     def finish(pair, carry):
         stacked = []
@@ -350,18 +377,56 @@
         out_ref[2 * pair + 1] = result[:, 128:]
         return carry
 
-    lax.fori_loop(0, capacity // 2, finish, 0, unroll=2)
-
+    for copy in out_copies:
+        copy.wait()
     for step in range(3):
         for half in range(2):
-            for which in order:
-                if (step, half) != (0, 0):
-                    halo_copy(step, half, which).wait_send()
+            if (step, half) != (0, 0):
+                halo_whole(step, half).wait_send()
     for which in range(2):
-        for k in range(1, GROUP):
-            within_copy(which, k).wait_send()
-        for k in range(1, groups):
-            across_copy(which, k).wait_send()
+        sum_whole(which, within).wait_send()
+        sum_whole(which, across).wait_send()
+
+
+def finish(
+    factor_hbm, high_hbm, low_hbm, out_hbm, factor_ref, high, low, out,
+    factor_sem, in_sem, out_sem,
+):
+    size = high.shape[0] // PARTS
+    pieces = [pl.ds(c * size, size) for c in range(PARTS)]
+    reads = [
+        [
+            pltpu.make_async_copy(high_hbm.at[piece], high.at[piece], in_sem.at[0, c]),
+            pltpu.make_async_copy(low_hbm.at[piece], low.at[piece], in_sem.at[1, c]),
+        ]
+        for c, piece in enumerate(pieces)
+    ]
+    writes = [
+        pltpu.make_async_copy(out.at[piece], out_hbm.at[piece], out_sem.at[c])
+        for c, piece in enumerate(pieces)
+    ]
+    factor_copy = pltpu.make_async_copy(factor_hbm, factor_ref, factor_sem)
+    factor_copy.start()
+    for pair in reads:
+        for copy in pair:
+            copy.start()
+    factor_copy.wait()
+    factor = factor_ref[...]
+    for c in range(PARTS):
+        for copy in reads[c]:
+            copy.wait()
+        for b in range(c * size, (c + 1) * size, 2):
+            stacked = [
+                jnp.concatenate([high[i], high[i], low[i], low[i]], axis=0) for i in (b, b + 1)
+            ]
+            result = jnp.dot(
+                factor, jnp.concatenate(stacked, axis=1), preferred_element_type=F32
+            )
+            out[b] = result[:, :128]
+            out[b + 1] = result[:, 128:]
+        writes[c].start()
+    for copy in writes:
+        copy.wait()
 
 
 def shards(
@@ -372,7 +437,6 @@
     fan = tile_columns.shape[1]
     _, neighbours, count = send_lists.shape
     groups = n // GROUP
-    sums = 2 * (GROUP - 1 + groups - 1)
     smem = pl.BlockSpec(memory_space=pltpu.SMEM)
     vmem = pl.BlockSpec(memory_space=pltpu.VMEM)
     hbm = pl.BlockSpec(memory_space=pl.ANY)
@@ -382,11 +446,12 @@
     wide = pltpu.VMEM((2, capacity, half, rows), F32)
     stacked = pltpu.VMEM((capacity, 2 * vectors, rows), BF16)
     scale = math.sqrt(capacity * n * rows)
-    return pl.pallas_call(
+    factor, high, low = pl.pallas_call(
         functools.partial(kernel, n, scale),
-        out_shape=jax.ShapeDtypeStruct((capacity, vectors, rows), F32),
+        out_shape=[jax.ShapeDtypeStruct((vectors, 256), BF16)]
+        + [jax.ShapeDtypeStruct((capacity, 2 * vectors, rows), BF16)] * 2,
         in_specs=[smem, smem, smem, smem, vmem, hbm, hbm],
-        out_specs=vmem,
+        out_specs=[vmem, hbm, hbm],
         scratch_shapes=[
             pltpu.VMEM((capacity, fan * rows, rows), BF16),
             pltpu.VMEM((capacity, vectors, rows), F32),
@@ -403,10 +468,11 @@
             pltpu.VMEM((2 * (groups - 1), 16, 128), F32),
             pltpu.SemaphoreType.DMA((CHUNKS,)),
             pltpu.SemaphoreType.DMA,
-            pltpu.SemaphoreType.DMA((6 * neighbours,)),
-            pltpu.SemaphoreType.DMA((6 * neighbours,)),
-            pltpu.SemaphoreType.DMA((sums,)),
-            pltpu.SemaphoreType.DMA((sums,)),
+            pltpu.SemaphoreType.DMA((2,)),
+            pltpu.SemaphoreType.DMA((6,)),
+            pltpu.SemaphoreType.DMA((6,)),
+            pltpu.SemaphoreType.DMA((4,)),
+            pltpu.SemaphoreType.DMA((4,)),
         ],
         compiler_params=pltpu.CompilerParams(
             collective_id=0, has_side_effects=True, vmem_limit_bytes=64 * 1024 * 1024
@@ -421,6 +487,23 @@
         tiles.reshape(capacity, fan * rows, rows),
         previous_block,
     )
+    return pl.pallas_call(
+        finish,
+        out_shape=jax.ShapeDtypeStruct((capacity, vectors, rows), F32),
+        in_specs=[hbm, hbm, hbm],
+        out_specs=hbm,
+        scratch_shapes=[
+            pltpu.VMEM((vectors, 256), BF16),
+            stacked,
+            stacked,
+            pltpu.VMEM((capacity, vectors, rows), F32),
+            pltpu.SemaphoreType.DMA,
+            pltpu.SemaphoreType.DMA((2, PARTS)),
+            pltpu.SemaphoreType.DMA((PARTS,)),
+        ],
+        compiler_params=pltpu.CompilerParams(vmem_limit_bytes=64 * 1024 * 1024),
+        name="finish",
+    )(factor, high, low)
 
 
 def solution(mesh):

time: 66.1 us -> 64 us (0.968)
  local copies, waits for them, and re-layouts: 2.06 us -> 0 us
    unnamed x1 -> x0, local copies, waits for them, and re-layouts: 2.06 us -> none
    pallas_call x1 -> x2, Pallas kernels: 63.2 us -> 63.2 us  [the longest x1 60.1 us: shards(): pl.pallas_call(functools.partial(kernel, n, scale), out_shape=[jax.ShapeD...]
where the time goes in v2:
time: 64 us; the launch traced here: 63.8 us
  Pallas kernels  63.2 us (99%)
  between operations  0.66 us (1%)
    pallas_call x1, Pallas kernels, shards(): pl.pallas_call(functools.partial(kernel, n, scale), out_shape=[jax.ShapeD...  60.1 us
    pallas_call x1, Pallas kernels, shards(): pl.pallas_call(finish, out_shape=jax.ShapeDtypeStruct((capacity, vectors,...  3.01 us

profile of v2, /device:TPU:0, one launch (start us, length us, event | category | flops | bytes accessed | tf_op | source)
XLA Modules:
  0.0 63.8 jit_solution(17931341600267439702)
XLA Ops:
  0.7 60.1 %filtered_step.1 = (bf16[32,256]{1,0:T(8,128)(2,1)}, bf16[48,64,128]{2,1,0:T(8,128)(2,1)}, bf16[48,64,128]{2,1,0:T(8,128)(2,1)}) custom-call(s32[1]{0:T(128)S(6)} %copy.8.live_ref, s32[12,48]{1,0:T(8,128)} %bitcast.4, s32[6,1,16]{2,1,0:T(1,128)} %bitcast.5, f32[4]{0:T(128)} %coeff_ref.1, bf16[48,32,128]{2,1,0:T(8,128)(2,1)} %start_ref.1, ...), custom_call_target="tpu_custom_call" | custom-call | tf_op jit(solution)/shard_map/filtered_step/pallas_call | solution.py:449
  60.8 3.0 %finish.1 = f32[48,32,128]{2,1,0:T(8,128)} custom-call(bf16[32,256]{1,0:T(8,128)(2,1)} %get-tuple-element.8.factor_hbm, bf16[48,64,128]{2,1,0:T(8,128)(2,1)} %get-tuple-element.9.high_hbm, bf16[48,64,128]{2,1,0:T(8,128)(2,1)} %get-tuple-element.10.low_hbm), custom_call_target="tpu_custom_call" | custom-call | tf_op jit(solution)/shard_map/finish/pallas_call | solution.py:490

commit v3 on v2

--- a/solution.py
+++ b/solution.py
@@ -61,11 +61,11 @@
 
 
 def kernel(
-    n, scale, live_ref, cols_ref, sends_ref, coeff_ref, start_ref, tiles_hbm, prev_hbm,
+    n, scale, live_hbm, cols_hbm, sends_hbm, coeff_hbm, start_hbm, tiles_hbm, prev_hbm,
     factor_ref, high_hbm, low_hbm,
-    tiles, prev, ext_a0, ext_b0, ext_a1, ext_b1, ext_a2, ext_b2, own_a1, own_b1, own_a2, own_b2,
+    live_ref, cols_ref, sends_ref, coeff_ref, start_ref, tiles, prev, ext_a0, ext_b0, ext_a1, ext_b1, ext_a2, ext_b2, own_a1, own_b1, own_a2, own_b2,
     outgoing, first, accum, y_high, y_low, inverse, mine, within, across,
-    tile_sem, prev_sem, out_sem, halo_send, halo_recv, sum_send, sum_recv,
+    entry_sem, tile_sem, prev_sem, out_sem, halo_send, halo_recv, sum_send, sum_recv,
 ):
     capacity = start_ref.shape[0]
     fan = cols_ref.shape[0]
@@ -75,17 +75,6 @@
     me = lax.axis_index("rows")
     ext = [[ext_a0, ext_b0], [ext_a1, ext_b1], [ext_a2, ext_b2]]
     own = [None, [own_a1, own_b1], [own_a2, own_b2]]
-    live = live_ref[0]
-
-    prev_copy = pltpu.make_async_copy(prev_hbm, prev, prev_sem)
-    prev_copy.start()
-    tile_copies = []
-    for c in range(CHUNKS):
-        piece = pl.ds(c * size, size)
-        copy = pltpu.make_async_copy(tiles_hbm.at[piece], tiles.at[piece], tile_sem.at[c])
-        copy.start()
-        tile_copies.append(copy)
-
     def halo_target(which):
         return lax.rem(me + shift_amount(which) + n, n)
 
@@ -101,6 +90,33 @@
     partners += [other_group(k) for k in range(1, groups)]
     for partner in partners:
         pl.semaphore_signal(barrier, inc=1, device_id=(partner,), device_id_type=MESH)
+
+    def entry_copy(source, target, which):
+        return pltpu.make_async_copy(source, target, entry_sem.at[which])
+
+    entries = [
+        entry_copy(*pair, i)
+        for i, pair in enumerate(
+            [
+                (sends_hbm, sends_ref),
+                (start_hbm, start_ref),
+                (live_hbm, live_ref),
+                (cols_hbm, cols_ref),
+                (coeff_hbm, coeff_ref),
+            ]
+        )
+    ]
+    prev_copy = pltpu.make_async_copy(prev_hbm, prev, prev_sem)
+    tile_copies = []
+    for c in range(CHUNKS):
+        piece = pl.ds(c * size, size)
+        tile_copies.append(
+            pltpu.make_async_copy(tiles_hbm.at[piece], tiles.at[piece], tile_sem.at[c])
+        )
+    for copy in entries:
+        copy.start()
+    prev_copy.start()
+    tile_copies[0].start()
 
     def gather(step, half, which):
         base = ((step * 2 + half) * neighbours + which) * count
@@ -134,12 +150,18 @@
         )
 
     order = (4, 5, 2, 3, 0, 1)
+    entries[0].wait()
+    entries[1].wait()
     for half in range(2):
         for which in order:
             gather(0, half, which)
     pl.semaphore_wait(barrier, len(partners))
     for which in order:
         halo_copy(0, 0, which).start()
+
+    for copy in entries[2:]:
+        copy.wait()
+    live = live_ref[0]
 
     def mask(b):
         return jnp.where(b < live, 1.0, 0.0).astype(F32)
@@ -210,6 +232,8 @@
     )
 
     prev_copy.wait()
+    for copy in tile_copies[1:]:
+        copy.start()
 
     def prev_gram(pair, total):
         left, right = [], []
@@ -437,7 +461,6 @@
     fan = tile_columns.shape[1]
     _, neighbours, count = send_lists.shape
     groups = n // GROUP
-    smem = pl.BlockSpec(memory_space=pltpu.SMEM)
     vmem = pl.BlockSpec(memory_space=pltpu.VMEM)
     hbm = pl.BlockSpec(memory_space=pl.ANY)
     half = vectors // 2
@@ -450,9 +473,14 @@
         functools.partial(kernel, n, scale),
         out_shape=[jax.ShapeDtypeStruct((vectors, 256), BF16)]
         + [jax.ShapeDtypeStruct((capacity, 2 * vectors, rows), BF16)] * 2,
-        in_specs=[smem, smem, smem, smem, vmem, hbm, hbm],
+        in_specs=[hbm] * 7,
         out_specs=[vmem, hbm, hbm],
         scratch_shapes=[
+            pltpu.SMEM(live_blocks.shape, jnp.int32),
+            pltpu.SMEM((fan, capacity), jnp.int32),
+            pltpu.SMEM((neighbours, 1, count), jnp.int32),
+            pltpu.SMEM(filter_coeffs.shape, F32),
+            pltpu.VMEM((capacity, vectors, rows), BF16),
             pltpu.VMEM((capacity, fan * rows, rows), BF16),
             pltpu.VMEM((capacity, vectors, rows), F32),
             *[extended] * 6,
@@ -466,6 +494,7 @@
             pltpu.VMEM((4, 16, 128), F32),
             pltpu.VMEM((2 * (GROUP - 1), 16, 128), F32),
             pltpu.VMEM((2 * (groups - 1), 16, 128), F32),
+            pltpu.SemaphoreType.DMA((5,)),
             pltpu.SemaphoreType.DMA((CHUNKS,)),
             pltpu.SemaphoreType.DMA,
             pltpu.SemaphoreType.DMA((2,)),

time: 64 us -> 61.5 us (0.961)
  Pallas kernels: 63.2 us -> 60.6 us
    pallas_call x1, Pallas kernels: 60.1 us -> 57.6 us  [shards(): pl.pallas_call(functools.partial(kernel, n, scale), out_shape=[jax.ShapeD...]
where the time goes in v3:
time: 61.5 us; the launch traced here: 61.3 us
  Pallas kernels  60.6 us (99%)
  between operations  0.66 us (1%)
    pallas_call x1, Pallas kernels, shards(): pl.pallas_call(functools.partial(kernel, n, scale), out_shape=[jax.ShapeD...  57.6 us
    pallas_call x1, Pallas kernels, shards(): pl.pallas_call(finish, out_shape=jax.ShapeDtypeStruct((capacity, vectors,...  3.01 us

profile of v3, /device:TPU:0, one launch (start us, length us, event | category | flops | bytes accessed | tf_op | source)
XLA Modules:
  0.0 61.3 jit_solution(10017140949446037717)
XLA Ops:
  0.7 57.6 %filtered_step.1 = (bf16[32,256]{1,0:T(8,128)(2,1)}, bf16[48,64,128]{2,1,0:T(8,128)(2,1)}, bf16[48,64,128]{2,1,0:T(8,128)(2,1)}) custom-call(s32[1]{0:T(128)S(6)} %copy.8.live_hbm, s32[12,48]{1,0:T(8,128)} %bitcast.4, s32[6,1,16]{2,1,0:T(1,128)} %bitcast.5, f32[4]{0:T(128)} %coeff_hbm.1, bf16[48,32,128]{2,1,0:T(8,128)(2,1)} %start_hbm.1, ...), custom_call_target="tpu_custom_call" | custom-call | tf_op jit(solution)/shard_map/filtered_step/pallas_call | solution.py:472
  58.3 3.0 %finish.1 = f32[48,32,128]{2,1,0:T(8,128)} custom-call(bf16[32,256]{1,0:T(8,128)(2,1)} %get-tuple-element.8.factor_hbm, bf16[48,64,128]{2,1,0:T(8,128)(2,1)} %get-tuple-element.9.high_hbm, bf16[48,64,128]{2,1,0:T(8,128)(2,1)} %get-tuple-element.10.low_hbm), custom_call_target="tpu_custom_call" | custom-call | tf_op jit(solution)/shard_map/finish/pallas_call | solution.py:519

commit v4 on v3

--- a/solution.py
+++ b/solution.py
@@ -13,7 +13,8 @@
 GROUP = 8
 PIVOTS = 8
 PARTS = 4
-UNROLL = 3
+BLOCKS = 24
+SPAN = 12
 CHUNKS = 8
 F32, BF16 = jnp.float32, jnp.bfloat16
 
@@ -107,16 +108,13 @@
         )
     ]
     prev_copy = pltpu.make_async_copy(prev_hbm, prev, prev_sem)
-    tile_copies = []
-    for c in range(CHUNKS):
+
+    def tile_copy(c):
         piece = pl.ds(c * size, size)
-        tile_copies.append(
-            pltpu.make_async_copy(tiles_hbm.at[piece], tiles.at[piece], tile_sem.at[c])
-        )
+        return pltpu.make_async_copy(tiles_hbm.at[piece], tiles.at[piece], tile_sem.at[c])
+
     for copy in entries:
         copy.start()
-    prev_copy.start()
-    tile_copies[0].start()
 
     def gather(step, half, which):
         base = ((step * 2 + half) * neighbours + which) * count
@@ -152,6 +150,8 @@
     order = (4, 5, 2, 3, 0, 1)
     entries[0].wait()
     entries[1].wait()
+    prev_copy.start()
+    tile_copy(0).start()
     for half in range(2):
         for which in order:
             gather(0, half, which)
@@ -232,8 +232,8 @@
     )
 
     prev_copy.wait()
-    for copy in tile_copies[1:]:
-        copy.start()
+    for c in range(1, CHUNKS):
+        tile_copy(c).start()
 
     def prev_gram(pair, total):
         left, right = [], []
@@ -253,63 +253,51 @@
     for which in order:
         halo_copy(0, 1, which).start()
 
-    def products(step, half, b):
+    def product(step, half, b):
         vectors = ext[step][half]
-        picked = [
-            jnp.concatenate([vectors[cols_ref[k, row]] for k in range(fan)], axis=1)
-            for row in (b, b + 1)
-        ]
-        result = jnp.dot(
-            jnp.concatenate(picked, axis=0),
-            jnp.concatenate([tiles[b], tiles[b + 1]], axis=1),
-            preferred_element_type=F32,
-        )
-        return result[:16, :128] * mask(b), result[16:, 128:] * mask(b + 1)
+        picked = jnp.concatenate([vectors[cols_ref[k, b]] for k in range(fan)], axis=1)
+        return jnp.dot(picked, tiles[b], preferred_element_type=F32) * mask(b)
 
     c0, c1, c2, c3 = (coeff_ref[i] for i in range(4))
 
     def first_step(half, b):
-        for i, result in enumerate(products(0, half, b)):
-            rounded = result.astype(BF16)
-            first[half, b + i] = result
-            own[1][half][b + i] = rounded
-            ext[1][half][b + i] = rounded
+        result = product(0, half, b)
+        rounded = result.astype(BF16)
+        first[half, b] = result
+        own[1][half][b] = rounded
+        ext[1][half][b] = rounded
 
     def second_step(half, b):
-        for i, result in enumerate(products(1, half, b)):
-            before = ext[0][half][b + i].astype(F32)
-            one = first[half, b + i]
-            result = 2.0 * result - before
-            rounded = result.astype(BF16)
-            own[2][half][b + i] = rounded
-            ext[2][half][b + i] = rounded
-            accum[half, b + i] = c0 * before + (c1 - c3) * one + c2 * result
+        before = ext[0][half][b].astype(F32)
+        one = first[half, b]
+        result = 2.0 * product(1, half, b) - before
+        rounded = result.astype(BF16)
+        own[2][half][b] = rounded
+        ext[2][half][b] = rounded
+        accum[half, b] = c0 * before + (c1 - c3) * one + c2 * result
 
     def third_step(half, b):
         rows = slice(32 + 16 * half, 48 + 16 * half)
-        for i, result in enumerate(products(2, half, b)):
-            high, low = split(accum[half, b + i] + (2.0 * c3) * result)
-            y_high[b + i, rows] = high
-            y_low[b + i, rows] = low
+        high, low = split(accum[half, b] + (2.0 * c3) * product(2, half, b))
+        y_high[b, rows] = high
+        y_low[b, rows] = low
 
     def await_halo(step, half):
         halo_whole(step, half).wait_recv()
 
     def loop(body, lower, upper):
-        def pair(i, carry):
-            body(lower + 2 * i)
+        def one(b, carry):
+            body(b)
             return carry
 
-        lax.fori_loop(0, (upper - lower) // 2, pair, 0, unroll=UNROLL)
+        lax.fori_loop(lower, upper, one, 0, unroll=BLOCKS)
 
     for half in range(2):
         await_halo(0, half)
-        for c in range(CHUNKS):
-            if half == 0:
-                tile_copies[c].wait()
-                loop(functools.partial(first_step, half), c * size, (c + 1) * size)
-        if half == 1:
-            loop(functools.partial(first_step, half), 0, capacity)
+        if half == 0:
+            for c in range(CHUNKS):
+                tile_copy(c).wait()
+        loop(functools.partial(first_step, half), 0, capacity)
         for which in order:
             gather(1, half, which)
             halo_copy(1, half, which).start()
@@ -331,16 +319,14 @@
             halo_copy(2, half, which).start()
 
     await_halo(2, 0)
-    span = 2 * UNROLL
-
     def third_group(half, group):
-        for i in range(UNROLL):
-            third_step(half, group * span + 2 * i)
+        for i in range(SPAN):
+            third_step(half, group * SPAN + i)
 
     def filtered_gram(group, total):
-        for i in range(UNROLL):
+        for i in range(0, SPAN, 2):
             left, right = [], []
-            for b in (group * span + 2 * i, group * span + 2 * i + 1):
+            for b in (group * SPAN + i, group * SPAN + i + 1):
                 left.append(jnp.concatenate([y_high[b, 32:64], y_low[b, 32:64]], axis=0))
                 right.append(jnp.concatenate([y_high[b], y_low[b]], axis=0))
             total += rows_dot(
@@ -356,8 +342,8 @@
     loop(functools.partial(third_step, 0), 0, capacity)
     await_halo(2, 1)
     third_group(1, 0)
-    total = lax.fori_loop(1, capacity // span, last_group, jnp.zeros((64, 128), F32))
-    total = filtered_gram(capacity // span - 1, total)
+    total = lax.fori_loop(1, capacity // SPAN, last_group, jnp.zeros((64, 128), F32))
+    total = filtered_gram(capacity // SPAN - 1, total)
     out_copies = [
         pltpu.make_async_copy(y_high, high_hbm, out_sem.at[0]),
         pltpu.make_async_copy(y_low, low_hbm, out_sem.at[1]),

time: 61.5 us -> 59.7 us (0.971)
  Pallas kernels: 60.6 us -> 58.9 us
    pallas_call x1, Pallas kernels: 57.6 us -> 55.8 us  [shards(): pl.pallas_call(functools.partial(kernel, n, scale), out_shape=[jax.ShapeD...]
where the time goes in v4:
time: 59.7 us; the launch traced here: 59.5 us
  Pallas kernels  58.9 us (99%)
  between operations  0.66 us (1%)
    pallas_call x1, Pallas kernels, shards(): pl.pallas_call(functools.partial(kernel, n, scale), out_shape=[jax.ShapeD...  55.8 us
    pallas_call x1, Pallas kernels, shards(): pl.pallas_call(finish, out_shape=jax.ShapeDtypeStruct((capacity, vectors,...  3.01 us

profile of v4, /device:TPU:0, one launch (start us, length us, event | category | flops | bytes accessed | tf_op | source)
XLA Modules:
  0.0 59.5 jit_solution(16545442830164045548)
XLA Ops:
  0.7 55.8 %filtered_step.1 = (bf16[32,256]{1,0:T(8,128)(2,1)}, bf16[48,64,128]{2,1,0:T(8,128)(2,1)}, bf16[48,64,128]{2,1,0:T(8,128)(2,1)}) custom-call(s32[1]{0:T(128)S(6)} %copy.8.live_hbm, s32[12,48]{1,0:T(8,128)} %bitcast.4, s32[6,1,16]{2,1,0:T(1,128)} %bitcast.5, f32[4]{0:T(128)} %coeff_hbm.1, bf16[48,32,128]{2,1,0:T(8,128)(2,1)} %start_hbm.1, ...), custom_call_target="tpu_custom_call" | custom-call | tf_op jit(solution)/shard_map/filtered_step/pallas_call | solution.py:458
  56.5 3.0 %finish.1 = f32[48,32,128]{2,1,0:T(8,128)} custom-call(bf16[32,256]{1,0:T(8,128)(2,1)} %get-tuple-element.8.factor_hbm, bf16[48,64,128]{2,1,0:T(8,128)(2,1)} %get-tuple-element.9.high_hbm, bf16[48,64,128]{2,1,0:T(8,128)(2,1)} %get-tuple-element.10.low_hbm), custom_call_target="tpu_custom_call" | custom-call | tf_op jit(solution)/shard_map/finish/pallas_call | solution.py:505

commit v5 on v4

v5 whole, which is shorter than its diff:
```python
import functools
import math

import jax
import jax.numpy as jnp
from jax import lax
from jax.experimental import pallas as pl
from jax.experimental.pallas import tpu as pltpu
from jax.sharding import PartitionSpec as P

MESH = pl.DeviceIdType.MESH
HIGHEST = lax.Precision.HIGHEST
GROUP = 8
PIVOTS = 8
PARTS = 3
BLOCKS = 24
SPAN = 24
CHUNKS = 8
F32, BF16 = jnp.float32, jnp.bfloat16

rows_dot = functools.partial(
    lax.dot_general, dimension_numbers=(((1,), (1,)), ((), ())), preferred_element_type=F32
)


def shift_amount(which):
    return (which // 2 + 1) * (1 if which % 2 == 0 else -1)


def iota(axis):
    return lax.broadcasted_iota(jnp.int32, (32, 128), axis)


def split(value):
    high = value.astype(BF16)
    return high, (value - high.astype(F32)).astype(BF16)


def eliminate(matrix, full):
    rows = iota(0)
    diagonal = jnp.zeros((32, 128), F32)
    for start in range(0, 32, PIVOTS):
        columns = [
            jnp.broadcast_to(matrix[:, j : j + 1], (32, 128))
            for j in range(start, start + PIVOTS)
        ]
        for p in range(PIVOTS):
            j = start + p
            row, column = matrix[j : j + 1, :], columns[p]
            keep = (rows != j) if full else (rows > j)
            factor = jnp.where(keep, column * (1.0 / column[j : j + 1, :]), 0.0)
            diagonal = jnp.where(rows == j, column, diagonal)
            matrix = matrix - factor * row
            for q in range(p + 1, PIVOTS):
                columns[q] = columns[q] - factor * columns[q][j : j + 1, :]
    return matrix, diagonal


def pack(total):
    folded = total + pltpu.roll(total, 64, 1)
    return jnp.where(iota(1)[:16] < 64, folded[:16], folded[16:])


def unpack(packed):
    return jnp.concatenate([packed, pltpu.roll(packed, 64, 1)], axis=0)


def solve(scale, state):
    rows, lanes = iota(0), iota(1)
    sums = state[32:]
    cross = jnp.where(lanes < 32, sums, 0.0)
    below = jnp.zeros((96, 128), F32)
    coeff = jnp.dot(
        cross, jnp.concatenate([state[:32], below], axis=0),
        precision=HIGHEST, preferred_element_type=F32,
    )
    removed = rows_dot(
        coeff, jnp.concatenate([pltpu.roll(cross, 32, 1), below], axis=0), precision=HIGHEST
    )
    matrix = jnp.where(
        lanes < 32,
        pltpu.roll(sums, 96, 1) - removed,
        jnp.where(lanes < 64, -coeff, jnp.where(lanes == rows + 64, 1.0, 0.0)),
    )
    matrix, diagonal = eliminate(matrix, False)
    factor = pltpu.roll(matrix * (scale * lax.rsqrt(diagonal)), 96, 1)
    factor = jnp.where(lanes < 64, factor, 0.0)
    high = factor.astype(BF16).astype(F32)
    both = jnp.where(lanes < 64, high, pltpu.roll(factor - high, 64, 1)).astype(BF16)
    return jnp.concatenate([both, both], axis=1)


def kernel(
    n, live_hbm, cols_hbm, sends_hbm, coeff_hbm, start_hbm, tiles_hbm, prev_hbm,
    state_ref, high_hbm, low_hbm,
    live_ref, cols_ref, sends_ref, coeff_ref, start_ref, tiles, prev, ext_a0, ext_b0, ext_a1, ext_b1, ext_a2, ext_b2, own_a1, own_b1, own_a2, own_b2,
    outgoing, first, accum, y_high, y_low, mine, within, across,
    entry_sem, tile_sem, prev_sem, out_sem, halo_send, halo_recv, sum_send, sum_recv,
):
    capacity = start_ref.shape[0]
    fan = cols_ref.shape[0]
    size = capacity // CHUNKS
    neighbours, _, count = sends_ref.shape
    groups = n // GROUP
    me = lax.axis_index("rows")
    ext = [[ext_a0, ext_b0], [ext_a1, ext_b1], [ext_a2, ext_b2]]
    own = [None, [own_a1, own_b1], [own_a2, own_b2]]
    def halo_target(which):
        return lax.rem(me + shift_amount(which) + n, n)

    def group_mate(k):
        return me // GROUP * GROUP + lax.rem(lax.rem(me, GROUP) + k, GROUP)

    def other_group(k):
        return lax.rem(me + k * GROUP, n)

    barrier = pltpu.get_barrier_semaphore()
    partners = [halo_target(w) for w in range(neighbours)]
    partners += [group_mate(k) for k in range(1, GROUP)]
    partners += [other_group(k) for k in range(1, groups)]
    for partner in partners:
        pl.semaphore_signal(barrier, inc=1, device_id=(partner,), device_id_type=MESH)

    def entry_copy(source, target, which):
        return pltpu.make_async_copy(source, target, entry_sem.at[which])

    entries = [
        entry_copy(*pair, i)
        for i, pair in enumerate(
            [
                (sends_hbm, sends_ref),
                (start_hbm, start_ref),
                (live_hbm, live_ref),
                (cols_hbm, cols_ref),
                (coeff_hbm, coeff_ref),
            ]
        )
    ]
    prev_copy = pltpu.make_async_copy(prev_hbm, prev, prev_sem)

    def tile_copy(c):
        piece = pl.ds(c * size, size)
        return pltpu.make_async_copy(tiles_hbm.at[piece], tiles.at[piece], tile_sem.at[c])

    for copy in entries:
        copy.start()

    def gather(step, half, which):
        base = ((step * 2 + half) * neighbours + which) * count
        for s in range(count):
            index = sends_ref[which, 0, s]
            if step == 0:
                outgoing[base + s] = start_ref[index, half * 16 : half * 16 + 16]
            else:
                outgoing[base + s] = own[step][half][index]

    def halo_copy(step, half, which):
        slot = (step * 2 + half) * neighbours + which
        return pltpu.make_async_remote_copy(
            src_ref=outgoing.at[pl.ds(slot * count, count)],
            dst_ref=ext[step][half].at[pl.ds(capacity + which * count, count)],
            send_sem=halo_send.at[step * 2 + half],
            recv_sem=halo_recv.at[step * 2 + half],
            device_id=(halo_target(which),),
            device_id_type=MESH,
        )

    def halo_whole(step, half):
        ghosts = neighbours * count
        return pltpu.make_async_remote_copy(
            src_ref=outgoing.at[pl.ds((step * 2 + half) * ghosts, ghosts)],
            dst_ref=ext[step][half].at[pl.ds(capacity, ghosts)],
            send_sem=halo_send.at[step * 2 + half],
            recv_sem=halo_recv.at[step * 2 + half],
            device_id=(halo_target(0),),
            device_id_type=MESH,
        )

    order = (4, 5, 2, 3, 0, 1)
    entries[0].wait()
    entries[1].wait()
    prev_copy.start()
    tile_copy(0).start()
    for half in range(2):
        for which in order:
            gather(0, half, which)
    pl.semaphore_wait(barrier, len(partners))
    for which in order:
        halo_copy(0, 0, which).start()

    for copy in entries[2:]:
        copy.wait()
    live = live_ref[0]

    def mask(b):
        return jnp.where(b < live, 1.0, 0.0).astype(F32)

    def fill(b, carry):
        value = (start_ref[b].astype(F32) * mask(b)).astype(BF16)
        ext_a0[b] = value[:16]
        ext_b0[b] = value[16:]
        return carry

    lax.fori_loop(0, capacity, fill, 0, unroll=4)

    def within_copy(which, k):
        return pltpu.make_async_remote_copy(
            src_ref=mine.at[2 * which],
            dst_ref=within.at[which * (GROUP - 1) + k - 1],
            send_sem=sum_send.at[2 * which],
            recv_sem=sum_recv.at[2 * which],
            device_id=(group_mate(k),),
            device_id_type=MESH,
        )

    def across_copy(which, k):
        return pltpu.make_async_remote_copy(
            src_ref=mine.at[2 * which + 1],
            dst_ref=across.at[which * (groups - 1) + k - 1],
            send_sem=sum_send.at[2 * which + 1],
            recv_sem=sum_recv.at[2 * which + 1],
            device_id=(other_group(k),),
            device_id_type=MESH,
        )

    def sum_whole(which, landing):
        peers = landing.shape[0] // 2
        slot = 2 * which + (0 if landing is within else 1)
        return pltpu.make_async_remote_copy(
            src_ref=landing.at[pl.ds(which * peers, peers)],
            dst_ref=landing.at[pl.ds(which * peers, peers)],
            send_sem=sum_send.at[slot],
            recv_sem=sum_recv.at[slot],
            device_id=(group_mate(1),),
            device_id_type=MESH,
        )

    def sum_start(which, value):
        mine[2 * which] = value
        for k in range(1, GROUP):
            within_copy(which, k).start()

    def sum_middle(which):
        total = mine[2 * which]
        sum_whole(which, within).wait_recv()
        for k in range(1, GROUP):
            total += within[which * (GROUP - 1) + k - 1]
        mine[2 * which + 1] = total
        for k in range(1, groups):
            across_copy(which, k).start()

    def sum_end(which):
        total = mine[2 * which + 1]
        sum_whole(which, across).wait_recv()
        for k in range(1, groups):
            total += across[which * (groups - 1) + k - 1]
        return total

    prev_copy.wait()
    for c in range(1, CHUNKS):
        tile_copy(c).start()

    def prev_gram(pair, total):
        left, right = [], []
        for b in (2 * pair, 2 * pair + 1):
            high, low = split(prev[b] * mask(b))
            y_high[b, :32] = high
            y_low[b, :32] = low
            left.append(jnp.concatenate([high, low], axis=0))
            right.append(jnp.concatenate([high, high, low, low], axis=0))
        return total + rows_dot(
            jnp.concatenate(left, axis=1), jnp.concatenate(right, axis=1)
        )

    total = lax.fori_loop(0, capacity // 2, prev_gram, jnp.zeros((64, 128), F32), unroll=2)
    sum_start(0, pack(total[:32] + total[32:]))
    halo_whole(0, 0).wait_send()
    for which in order:
        halo_copy(0, 1, which).start()

    def product(step, half, b):
        vectors = ext[step][half]
        picked = jnp.concatenate([vectors[cols_ref[k, b]] for k in range(fan)], axis=1)
        return jnp.dot(picked, tiles[b], preferred_element_type=F32) * mask(b)

    c0, c1, c2, c3 = (coeff_ref[i] for i in range(4))

    def first_step(half, b):
        result = product(0, half, b)
        rounded = result.astype(BF16)
        first[half, b] = result
        own[1][half][b] = rounded
        ext[1][half][b] = rounded

    def second_step(half, b):
        before = ext[0][half][b].astype(F32)
        one = first[half, b]
        result = 2.0 * product(1, half, b) - before
        rounded = result.astype(BF16)
        own[2][half][b] = rounded
        ext[2][half][b] = rounded
        accum[half, b] = c0 * before + (c1 - c3) * one + c2 * result

    def third_step(half, b):
        rows = slice(32 + 16 * half, 48 + 16 * half)
        high, low = split(accum[half, b] + (2.0 * c3) * product(2, half, b))
        y_high[b, rows] = high
        y_low[b, rows] = low

    def await_halo(step, half):
        halo_whole(step, half).wait_recv()

    def loop(body, lower, upper):
        def one(b, carry):
            body(b)
            return carry

        lax.fori_loop(lower, upper, one, 0, unroll=BLOCKS)

    for half in range(2):
        await_halo(0, half)
        if half == 0:
            for c in range(CHUNKS):
                tile_copy(c).wait()
        loop(functools.partial(first_step, half), 0, capacity)
        for which in order:
            gather(1, half, which)
        if half == 0:
            halo_whole(0, 1).wait_send()
        for which in order:
            halo_copy(1, half, which).start()
        if half == 0:
            sum_middle(0)

    rows, lanes = iota(0), iota(1)
    gram = unpack(sum_end(0))
    matrix = jnp.where(lanes < 32, gram, jnp.where(lanes == rows + 64, 1.0, 0.0))
    matrix, diagonal = eliminate(matrix, True)
    middle = (lanes >= 32) & (lanes < 64)
    state_ref[:32] = jnp.where(middle, pltpu.roll(matrix / diagonal, 96, 1), 0.0)

    for half in range(2):
        await_halo(1, half)
        loop(functools.partial(second_step, half), 0, capacity)
        for which in order:
            gather(2, half, which)
            halo_copy(2, half, which).start()

    await_halo(2, 0)
    def third_group(half, group):
        for i in range(SPAN):
            third_step(half, group * SPAN + i)

    def filtered_gram(group, total):
        for i in range(0, SPAN, 2):
            left, right = [], []
            for b in (group * SPAN + i, group * SPAN + i + 1):
                left.append(jnp.concatenate([y_high[b, 32:64], y_low[b, 32:64]], axis=0))
                right.append(jnp.concatenate([y_high[b], y_low[b]], axis=0))
            total += rows_dot(
                jnp.concatenate(left, axis=1), jnp.concatenate(right, axis=1)
            )
        return total

    def last_group(group, total):
        total = filtered_gram(group - 1, total)
        third_group(1, group)
        return total

    loop(functools.partial(third_step, 0), 0, capacity)
    await_halo(2, 1)
    third_group(1, 0)
    total = lax.fori_loop(1, capacity // SPAN, last_group, jnp.zeros((64, 128), F32))
    total = filtered_gram(capacity // SPAN - 1, total)
    out_copies = [
        pltpu.make_async_copy(y_high, high_hbm, out_sem.at[0]),
        pltpu.make_async_copy(y_low, low_hbm, out_sem.at[1]),
    ]
    sum_start(1, pack(total[:32] + total[32:]))
    for copy in out_copies:
        copy.start()
    sum_middle(1)
    state_ref[32:] = unpack(sum_end(1))
    for copy in out_copies:
        copy.wait()
    for step in range(1, 3):
        for half in range(2):
            halo_whole(step, half).wait_send()
    for which in range(2):
        sum_whole(which, within).wait_send()
        sum_whole(which, across).wait_send()


def finish(
    scale, state_hbm, high_hbm, low_hbm, out_hbm, state, high, low, out,
    state_sem, in_sem, out_sem,
):
    size = high.shape[0] // PARTS
    pieces = [pl.ds(c * size, size) for c in range(PARTS)]
    reads = [
        [
            pltpu.make_async_copy(high_hbm.at[piece], high.at[piece], in_sem.at[0, c]),
            pltpu.make_async_copy(low_hbm.at[piece], low.at[piece], in_sem.at[1, c]),
        ]
        for c, piece in enumerate(pieces)
    ]
    writes = [
        pltpu.make_async_copy(out.at[piece], out_hbm.at[piece], out_sem.at[c])
        for c, piece in enumerate(pieces)
    ]
    state_copy = pltpu.make_async_copy(state_hbm, state, state_sem)
    state_copy.start()
    state_copy.wait()
    for pair in reads:
        for copy in pair:
            copy.start()
    factor = solve(scale, state[...])
    for c in range(PARTS):
        for copy in reads[c]:
            copy.wait()
        for b in range(c * size, (c + 1) * size, 2):
            stacked = [
                jnp.concatenate([high[i], high[i], low[i], low[i]], axis=0) for i in (b, b + 1)
            ]
            result = jnp.dot(
                factor, jnp.concatenate(stacked, axis=1), preferred_element_type=F32
            )
            out[b] = result[:, :128]
            out[b + 1] = result[:, 128:]
        writes[c].start()
    for copy in writes:
        copy.wait()


def shards(
    live_blocks, tile_columns, send_lists, tiles, filter_coeffs, start_block, previous_block
):
    n = lax.axis_size("rows")
    capacity, vectors, rows = start_block.shape
    fan = tile_columns.shape[1]
    _, neighbours, count = send_lists.shape
    groups = n // GROUP
    vmem = pl.BlockSpec(memory_space=pltpu.VMEM)
    hbm = pl.BlockSpec(memory_space=pl.ANY)
    half = vectors // 2
    field = pltpu.VMEM((capacity, half, rows), BF16)
    extended = pltpu.VMEM((capacity + neighbours * count, half, rows), BF16)
    wide = pltpu.VMEM((2, capacity, half, rows), F32)
    stacked = pltpu.VMEM((capacity, 2 * vectors, rows), BF16)
    scale = math.sqrt(capacity * n * rows)
    state, high, low = pl.pallas_call(
        functools.partial(kernel, n),
        out_shape=[jax.ShapeDtypeStruct((2 * vectors, 128), F32)]
        + [jax.ShapeDtypeStruct((capacity, 2 * vectors, rows), BF16)] * 2,
        in_specs=[hbm] * 7,
        out_specs=[vmem, hbm, hbm],
        scratch_shapes=[
            pltpu.SMEM(live_blocks.shape, jnp.int32),
            pltpu.SMEM((fan, capacity), jnp.int32),
            pltpu.SMEM((neighbours, 1, count), jnp.int32),
            pltpu.SMEM(filter_coeffs.shape, F32),
            pltpu.VMEM((capacity, vectors, rows), BF16),
            pltpu.VMEM((capacity, fan * rows, rows), BF16),
            pltpu.VMEM((capacity, vectors, rows), F32),
            *[extended] * 6,
            *[field] * 4,
            pltpu.VMEM((6 * neighbours * count, half, rows), BF16),
            wide,
            wide,
            stacked,
            stacked,
            pltpu.VMEM((4, 16, 128), F32),
            pltpu.VMEM((2 * (GROUP - 1), 16, 128), F32),
            pltpu.VMEM((2 * (groups - 1), 16, 128), F32),
            pltpu.SemaphoreType.DMA((5,)),
            pltpu.SemaphoreType.DMA((CHUNKS,)),
            pltpu.SemaphoreType.DMA,
            pltpu.SemaphoreType.DMA((2,)),
            pltpu.SemaphoreType.DMA((6,)),
            pltpu.SemaphoreType.DMA((6,)),
            pltpu.SemaphoreType.DMA((4,)),
            pltpu.SemaphoreType.DMA((4,)),
        ],
        compiler_params=pltpu.CompilerParams(
            collective_id=0, has_side_effects=True, vmem_limit_bytes=64 * 1024 * 1024
        ),
        name="filtered_step",
    )(
        live_blocks,
        tile_columns.T,
        jnp.transpose(send_lists, (1, 0, 2)),
        filter_coeffs,
        start_block,
        tiles.reshape(capacity, fan * rows, rows),
        previous_block,
    )
    return pl.pallas_call(
        functools.partial(finish, scale),
        out_shape=jax.ShapeDtypeStruct((capacity, vectors, rows), F32),
        in_specs=[hbm, hbm, hbm],
        out_specs=hbm,
        scratch_shapes=[
            pltpu.VMEM((2 * vectors, 128), F32),
            stacked,
            stacked,
            pltpu.VMEM((capacity, vectors, rows), F32),
            pltpu.SemaphoreType.DMA,
            pltpu.SemaphoreType.DMA((2, PARTS)),
            pltpu.SemaphoreType.DMA((PARTS,)),
        ],
        compiler_params=pltpu.CompilerParams(vmem_limit_bytes=64 * 1024 * 1024),
        name="finish",
    )(state, high, low)


def solution(mesh):
    return jax.shard_map(
        shards,
        mesh=mesh,
        in_specs=(
            P("rows"),
            P("rows", None),
            P("rows", None, None),
            P("rows", None, None, None),
            P(),
            P("rows", None, None),
            P("rows", None, None),
        ),
        out_specs=P("rows", None, None),
        check_vma=False,
    )
```

time: 59.7 us -> 59.1 us (0.990)
  Pallas kernels: 58.9 us -> 58.3 us
    pallas_call x2, Pallas kernels: 58.9 us -> 58.3 us  [the longest x1 54.1 us: shards(): pl.pallas_call(functools.partial(kernel, n), out_shape=[jax.ShapeDtypeStr...]
where the time goes in v5:
time: 59.1 us; the launch traced here: 58.9 us
  Pallas kernels  58.3 us (99%)
  between operations  0.66 us (1%)
    pallas_call x1, Pallas kernels, shards(): pl.pallas_call(functools.partial(kernel, n), out_shape=[jax.ShapeDtypeStr...  54.1 us
    pallas_call x1, Pallas kernels, shards(): pl.pallas_call(functools.partial(finish, scale), out_shape=jax.ShapeDtype...  4.15 us

profile of v5, /device:TPU:0, one launch (start us, length us, event | category | flops | bytes accessed | tf_op | source)
XLA Modules:
  0.0 58.9 jit_solution(6444503153594229124)
XLA Ops:
  0.7 54.1 %filtered_step.1 = (f32[64,128]{1,0:T(8,128)}, bf16[48,64,128]{2,1,0:T(8,128)(2,1)}, bf16[48,64,128]{2,1,0:T(8,128)(2,1)}) custom-call(s32[1]{0:T(128)S(6)} %copy.8.live_hbm, s32[12,48]{1,0:T(8,128)} %bitcast.4, s32[6,1,16]{2,1,0:T(1,128)} %bitcast.5, f32[4]{0:T(128)} %coeff_hbm.1, bf16[48,32,128]{2,1,0:T(8,128)(2,1)} %start_hbm.1, ...), custom_call_target="tpu_custom_call" | custom-call | tf_op jit(solution)/shard_map/filtered_step/pallas_call | solution.py:451
  54.8 4.1 %finish.1 = f32[48,32,128]{2,1,0:T(8,128)} custom-call(f32[64,128]{1,0:T(8,128)} %get-tuple-element.8.state_hbm, bf16[48,64,128]{2,1,0:T(8,128)(2,1)} %get-tuple-element.9.high_hbm, bf16[48,64,128]{2,1,0:T(8,128)(2,1)} %get-tuple-element.10.low_hbm), custom_call_target="tpu_custom_call" | custom-call | tf_op jit(solution)/shard_map/finish/pallas_call | solution.py:497

commit v6 on v5

--- a/solution.py
+++ b/solution.py
@@ -93,11 +93,11 @@
 def kernel(
     n, live_hbm, cols_hbm, sends_hbm, coeff_hbm, start_hbm, tiles_hbm, prev_hbm,
     state_ref, high_hbm, low_hbm,
-    live_ref, cols_ref, sends_ref, coeff_ref, start_ref, tiles, prev, ext_a0, ext_b0, ext_a1, ext_b1, ext_a2, ext_b2, own_a1, own_b1, own_a2, own_b2,
+    live_ref, cols_ref, sends_ref, coeff_ref, start_a, start_b, tiles, prev, ext_a0, ext_b0, ext_a1, ext_b1, ext_a2, ext_b2, own_a1, own_b1, own_a2, own_b2,
     outgoing, first, accum, y_high, y_low, mine, within, across,
     entry_sem, tile_sem, prev_sem, out_sem, halo_send, halo_recv, sum_send, sum_recv,
 ):
-    capacity = start_ref.shape[0]
+    capacity = start_a.shape[0]
     fan = cols_ref.shape[0]
     size = capacity // CHUNKS
     neighbours, _, count = sends_ref.shape
@@ -105,6 +105,25 @@
     me = lax.axis_index("rows")
     ext = [[ext_a0, ext_b0], [ext_a1, ext_b1], [ext_a2, ext_b2]]
     own = [None, [own_a1, own_b1], [own_a2, own_b2]]
+    def entry_copy(source, target, which):
+        return pltpu.make_async_copy(source, target, entry_sem.at[which])
+
+    entries = [
+        entry_copy(*pair, i)
+        for i, pair in enumerate(
+            [
+                (sends_hbm, sends_ref),
+                (start_hbm.at[:, :16], start_a),
+                (start_hbm.at[:, 16:], start_b),
+                (live_hbm, live_ref),
+                (cols_hbm, cols_ref),
+                (coeff_hbm, coeff_ref),
+            ]
+        )
+    ]
+    entries[0].start()
+    entries[1].start()
+
     def halo_target(which):
         return lax.rem(me + shift_amount(which) + n, n)
 
@@ -121,28 +140,13 @@
     for partner in partners:
         pl.semaphore_signal(barrier, inc=1, device_id=(partner,), device_id_type=MESH)
 
-    def entry_copy(source, target, which):
-        return pltpu.make_async_copy(source, target, entry_sem.at[which])
-
-    entries = [
-        entry_copy(*pair, i)
-        for i, pair in enumerate(
-            [
-                (sends_hbm, sends_ref),
-                (start_hbm, start_ref),
-                (live_hbm, live_ref),
-                (cols_hbm, cols_ref),
-                (coeff_hbm, coeff_ref),
-            ]
-        )
-    ]
     prev_copy = pltpu.make_async_copy(prev_hbm, prev, prev_sem)
 
     def tile_copy(c):
         piece = pl.ds(c * size, size)
         return pltpu.make_async_copy(tiles_hbm.at[piece], tiles.at[piece], tile_sem.at[c])
 
-    for copy in entries:
+    for copy in entries[2:]:
         copy.start()
 
     def gather(step, half, which):
@@ -150,7 +154,7 @@
         for s in range(count):
             index = sends_ref[which, 0, s]
             if step == 0:
-                outgoing[base + s] = start_ref[index, half * 16 : half * 16 + 16]
+                outgoing[base + s] = (start_b if half else start_a)[index]
             else:
                 outgoing[base + s] = own[step][half][index]
 
@@ -181,14 +185,16 @@
     entries[1].wait()
     prev_copy.start()
     tile_copy(0).start()
-    for half in range(2):
-        for which in order:
-            gather(0, half, which)
+    for which in order:
+        gather(0, 0, which)
     pl.semaphore_wait(barrier, len(partners))
     for which in order:
         halo_copy(0, 0, which).start()
-
-    for copy in entries[2:]:
+    entries[2].wait()
+    for which in order:
+        gather(0, 1, which)
+
+    for copy in entries[3:]:
         copy.wait()
     live = live_ref[0]
 
@@ -196,9 +202,8 @@
         return jnp.where(b < live, 1.0, 0.0).astype(F32)
 
     def fill(b, carry):
-        value = (start_ref[b].astype(F32) * mask(b)).astype(BF16)
-        ext_a0[b] = value[:16]
-        ext_b0[b] = value[16:]
+        ext_a0[b] = (start_a[b].astype(F32) * mask(b)).astype(BF16)
+        ext_b0[b] = (start_b[b].astype(F32) * mask(b)).astype(BF16)
         return carry
 
     lax.fori_loop(0, capacity, fill, 0, unroll=4)
@@ -459,7 +464,8 @@
             pltpu.SMEM((fan, capacity), jnp.int32),
             pltpu.SMEM((neighbours, 1, count), jnp.int32),
             pltpu.SMEM(filter_coeffs.shape, F32),
-            pltpu.VMEM((capacity, vectors, rows), BF16),
+            field,
+            field,
             pltpu.VMEM((capacity, fan * rows, rows), BF16),
             pltpu.VMEM((capacity, vectors, rows), F32),
             *[extended] * 6,
@@ -472,7 +478,7 @@
             pltpu.VMEM((4, 16, 128), F32),
             pltpu.VMEM((2 * (GROUP - 1), 16, 128), F32),
             pltpu.VMEM((2 * (groups - 1), 16, 128), F32),
-            pltpu.SemaphoreType.DMA((5,)),
+            pltpu.SemaphoreType.DMA((6,)),
             pltpu.SemaphoreType.DMA((CHUNKS,)),
             pltpu.SemaphoreType.DMA,
             pltpu.SemaphoreType.DMA((2,)),

time: 59.1 us -> 58.5 us (0.990)
  Pallas kernels: 58.3 us -> 57.7 us
where the time goes in v6:
time: 58.5 us; the launch traced here: 58.3 us
  Pallas kernels  57.7 us (99%)
  between operations  0.66 us (1%)
    pallas_call x1, Pallas kernels, shards(): pl.pallas_call(functools.partial(kernel, n), out_shape=[jax.ShapeDtypeStr...  53.5 us
    pallas_call x1, Pallas kernels, shards(): pl.pallas_call(functools.partial(finish, scale), out_shape=jax.ShapeDtype...  4.15 us

profile of v6, /device:TPU:0, one launch (start us, length us, event | category | flops | bytes accessed | tf_op | source)
XLA Modules:
  0.0 58.3 jit_solution(9110226371501614877)
XLA Ops:
  0.7 53.5 %filtered_step.1 = (f32[64,128]{1,0:T(8,128)}, bf16[48,64,128]{2,1,0:T(8,128)(2,1)}, bf16[48,64,128]{2,1,0:T(8,128)(2,1)}) custom-call(s32[1]{0:T(128)S(6)} %copy.8.live_hbm, s32[12,48]{1,0:T(8,128)} %bitcast.4, s32[6,1,16]{2,1,0:T(1,128)} %bitcast.5, f32[4]{0:T(128)} %coeff_hbm.1, bf16[48,32,128]{2,1,0:T(8,128)(2,1)} %start_hbm.1, ...), custom_call_target="tpu_custom_call" | custom-call | tf_op jit(solution)/shard_map/filtered_step/pallas_call | solution.py:456
  54.2 4.1 %finish.1 = f32[48,32,128]{2,1,0:T(8,128)} custom-call(f32[64,128]{1,0:T(8,128)} %get-tuple-element.8.state_hbm, bf16[48,64,128]{2,1,0:T(8,128)(2,1)} %get-tuple-element.9.high_hbm, bf16[48,64,128]{2,1,0:T(8,128)(2,1)} %get-tuple-element.10.low_hbm), custom_call_target="tpu_custom_call" | custom-call | tf_op jit(solution)/shard_map/finish/pallas_call | solution.py:503

commit v7 on v6

--- a/solution.py
+++ b/solution.py
@@ -415,10 +415,10 @@
     ]
     state_copy = pltpu.make_async_copy(state_hbm, state, state_sem)
     state_copy.start()
-    state_copy.wait()
     for pair in reads:
         for copy in pair:
             copy.start()
+    state_copy.wait()
     factor = solve(scale, state[...])
     for c in range(PARTS):
         for copy in reads[c]:

time: 58.5 us -> 58.4 us (level)
  no operation moved by 1% of the time
where the time goes in v7:
time: 58.4 us; the launch traced here: 58.3 us
  Pallas kernels  57.6 us (99%)
  between operations  0.66 us (1%)
    pallas_call x1, Pallas kernels, shards(): pl.pallas_call(functools.partial(kernel, n), out_shape=[jax.ShapeDtypeStr...  53.5 us
    pallas_call x1, Pallas kernels, shards(): pl.pallas_call(functools.partial(finish, scale), out_shape=jax.ShapeDtype...  4.05 us

profile of v7, /device:TPU:0, one launch (start us, length us, event | category | flops | bytes accessed | tf_op | source)
XLA Modules:
  0.0 58.3 jit_solution(8474692427582984341)
XLA Ops:
  0.7 53.5 %filtered_step.1 = (f32[64,128]{1,0:T(8,128)}, bf16[48,64,128]{2,1,0:T(8,128)(2,1)}, bf16[48,64,128]{2,1,0:T(8,128)(2,1)}) custom-call(s32[1]{0:T(128)S(6)} %copy.8.live_hbm, s32[12,48]{1,0:T(8,128)} %bitcast.4, s32[6,1,16]{2,1,0:T(1,128)} %bitcast.5, f32[4]{0:T(128)} %coeff_hbm.1, bf16[48,32,128]{2,1,0:T(8,128)(2,1)} %start_hbm.1, ...), custom_call_target="tpu_custom_call" | custom-call | tf_op jit(solution)/shard_map/filtered_step/pallas_call | solution.py:456
  54.2 4.1 %finish.1 = f32[48,32,128]{2,1,0:T(8,128)} custom-call(f32[64,128]{1,0:T(8,128)} %get-tuple-element.8.state_hbm, bf16[48,64,128]{2,1,0:T(8,128)(2,1)} %get-tuple-element.9.high_hbm, bf16[48,64,128]{2,1,0:T(8,128)(2,1)} %get-tuple-element.10.low_hbm), custom_call_target="tpu_custom_call" | custom-call | tf_op jit(solution)/shard_map/finish/pallas_call | solution.py:503

commit v8 on v7

--- a/solution.py
+++ b/solution.py
@@ -11,7 +11,7 @@
 MESH = pl.DeviceIdType.MESH
 HIGHEST = lax.Precision.HIGHEST
 GROUP = 8
-PIVOTS = 8
+PIVOTS = 16
 PARTS = 3
 BLOCKS = 24
 SPAN = 24

time: 58.4 us -> 58.2 us (level)
  no operation moved by 1% of the time
where the time goes in v8:
time: 58.2 us; the launch traced here: 58.1 us
  Pallas kernels  57.4 us (99%)
  between operations  0.66 us (1%)
    pallas_call x1, Pallas kernels, shards(): pl.pallas_call(functools.partial(kernel, n), out_shape=[jax.ShapeDtypeStr...  53.5 us
    pallas_call x1, Pallas kernels, shards(): pl.pallas_call(functools.partial(finish, scale), out_shape=jax.ShapeDtype...  3.93 us

profile of v8, /device:TPU:0, one launch (start us, length us, event | category | flops | bytes accessed | tf_op | source)
XLA Modules:
  0.0 58.1 jit_solution(4065903655836894830)
XLA Ops:
  0.7 53.5 %filtered_step.1 = (f32[64,128]{1,0:T(8,128)}, bf16[48,64,128]{2,1,0:T(8,128)(2,1)}, bf16[48,64,128]{2,1,0:T(8,128)(2,1)}) custom-call(s32[1]{0:T(128)S(6)} %copy.8.live_hbm, s32[12,48]{1,0:T(8,128)} %bitcast.4, s32[6,1,16]{2,1,0:T(1,128)} %bitcast.5, f32[4]{0:T(128)} %coeff_hbm.1, bf16[48,32,128]{2,1,0:T(8,128)(2,1)} %start_hbm.1, ...), custom_call_target="tpu_custom_call" | custom-call | tf_op jit(solution)/shard_map/filtered_step/pallas_call | solution.py:456
  54.1 3.9 %finish.1 = f32[48,32,128]{2,1,0:T(8,128)} custom-call(f32[64,128]{1,0:T(8,128)} %get-tuple-element.8.state_hbm, bf16[48,64,128]{2,1,0:T(8,128)(2,1)} %get-tuple-element.9.high_hbm, bf16[48,64,128]{2,1,0:T(8,128)(2,1)} %get-tuple-element.10.low_hbm), custom_call_target="tpu_custom_call" | custom-call | tf_op jit(solution)/shard_map/finish/pallas_call | solution.py:503
